TPU v7x, 512 devices: a whole 4x4x16 slice. The times are simulated.
512 devices in a mesh: blk: 8 (over y, x_hi), grp: 64 (over z, x_lo, core).
Axes of the slice: x: 4 (x_hi: 2, x_lo: 2; x = x_hi * 2 + x_lo), y: 4, z: 16, core: 2. Of those that a mesh axis runs over, the one named last changes fastest.
Arguments:
- positions: float32 [3, 131072], P(None, ('blk', 'grp')), may hold values from -6 to 6
- velocities: float32 [3, 131072], P(None, ('blk', 'grp')), may hold values from -6 to 6
- accelerations: float32 [3, 131072], P(None, ('blk', 'grp')), may hold values from -4 to 4
- jerks: float32 [3, 131072], P(None, ('blk', 'grp')), may hold values from -4 to 4
- mass_weight: float32 [131072], P(('blk', 'grp')), may hold values from 0.3 to 3
- levels: int32 [131072], P(('blk', 'grp')), may hold values from 0 to 3, as said below
- active: int32 [2, 12288], P(None, ('blk', 'grp')), may hold values from 0 to 255, as said below
- counts: int32 [2, 512], P(None, ('blk', 'grp')), may hold values from 1 to 24
Outputs:
- positions_out: float32 [3, 131072], P(None, ('blk', 'grp'))
- velocities_out: float32 [3, 131072], P(None, ('blk', 'grp'))
- accelerations_out: float32 [3, 131072], P(None, ('blk', 'grp'))
- jerks_out: float32 [3, 131072], P(None, ('blk', 'grp'))
- fresh_forces: float32 [2, 6, 12288], P(None, None, ('blk', 'grp'))
Inputs may be any that keep to these rules, and one draw needn't show every extreme that they name: `active`: entries are local indices of the owner's particles; the live slots of one owner's list are distinct, dead slots hold 0. `levels`: particles not named in any list have level 2 or 3.
All inputs are finite; a program needn't handle non-finite values.
Results may differ from a plain program's by a relative error of at most 0.0003.
Values sent between devices are 32-bit elements; how exact they have to be, the bound alone decides.
No kernel may reach another device: no remote copies, remote signals or barrier semaphores. Data moves between devices by JAX's collectives and lax.ppermute only.
A program may use at most 64 MiB of HBM per device.

v0:
```python
import jax
import jax.numpy as jnp
from jax import lax
from jax.sharding import PartitionSpec as P

STEP_BASE = 0.125
SOFTEN = 0.01


def passed_along(value, axis, steps):
    count = lax.axis_size(axis)
    pairs = [(source, (source + steps) % count) for source in range(count)]
    return lax.ppermute(value, axis, pairs)


def predict(pos, vel, acc, jerk, elapsed):
    pred_pos = pos + elapsed * (vel + elapsed * (acc * 0.5 + elapsed * jerk / 6.0))
    pred_vel = vel + elapsed * (acc + elapsed * jerk * 0.5)
    return (pred_pos, pred_vel)


def correct(pos, vel, acc, jerk, new_acc, new_jerk, stride, hit):
    half = 0.5 * stride
    square = stride * stride / 12.0
    vel_new = vel + half * (acc + new_acc) + square * (jerk - new_jerk)
    pos_new = pos + half * (vel + vel_new) + square * (acc - new_acc)
    return (
        jnp.where(hit, pos_new, pos),
        jnp.where(hit, vel_new, vel),
        jnp.where(hit, new_acc, acc),
        jnp.where(hit, new_jerk, jerk),
    )


def block_terms(iblock, jpart):
    dpos = jpart[0:3, :, None] - iblock[0:3, None, :]
    dvel = jpart[3:6, :, None] - iblock[3:6, None, :]
    dist = dpos[0] * dpos[0] + dpos[1] * dpos[1] + dpos[2] * dpos[2] + SOFTEN
    inverse = lax.rsqrt(dist)
    weight = jpart[6][:, None] * inverse * inverse * inverse
    radial = 3.0 * (dpos[0] * dvel[0] + dpos[1] * dvel[1] + dpos[2] * dvel[2]) * inverse * inverse
    accel = jnp.sum(weight[None] * dpos, axis=1)
    jerk = jnp.sum(weight[None] * (dvel - radial[None] * dpos), axis=1)
    return jnp.concatenate([accel, jerk], axis=0)


def pair_terms(ipart, jpart):
    rows = ipart.shape[1]
    width = 512
    blocks = ipart.reshape(6, rows // width, width).transpose(1, 0, 2)
    result = lax.map(lambda iblock: block_terms(iblock, jpart), blocks)
    return result.transpose(1, 0, 2).reshape(6, rows)


def body(positions, velocities, accelerations, jerks, mass_weight, levels, active, counts):
    count_part = positions.shape[1]
    loop_len = lax.axis_size("blk")
    total_part = count_part * loop_len * lax.axis_size("grp")
    mass = mass_weight / total_part
    clock = jnp.zeros((count_part,), jnp.float32)
    stride = STEP_BASE * jnp.left_shift(jnp.ones_like(levels), levels).astype(jnp.float32)
    particle = jnp.arange(count_part, dtype=jnp.int32)
    slot = jnp.arange(active.shape[1], dtype=jnp.int32)
    pos, vel, acc, jerk = (positions, velocities, accelerations, jerks)
    recorded = []
    for step in range(2):
        now = STEP_BASE * (step + 1)
        elapsed = now - clock
        pred_pos, pred_vel = predict(pos, vel, acc, jerk, elapsed)
        live = slot < counts[step, 0]
        picker = ((active[step][:, None] == particle[None, :]) & live[:, None]).astype(jnp.float32)
        pred_both = jnp.concatenate([pred_pos, pred_vel], axis=0)
        chosen = jnp.dot(pred_both, picker.T, precision=lax.Precision.HIGHEST)
        jdata = jnp.concatenate([pred_pos, pred_vel, mass[None, :]], axis=0)
        row_actives = lax.all_gather(chosen, "grp", axis=1, tiled=True)
        travel = jdata
        partial_value = pair_terms(row_actives, travel)
        for turn in range(loop_len - 1):
            travel = passed_along(travel, "blk", 1)
            partial_value = partial_value + pair_terms(row_actives, travel)
        fresh = lax.psum_scatter(partial_value, "grp", scatter_dimension=1, tiled=True)
        recorded.append(jnp.where(live[None, :], fresh, jnp.zeros_like(fresh)))
        spread = jnp.dot(fresh, picker, precision=lax.Precision.HIGHEST)
        hit = jnp.sum(picker, axis=0) > 0.5
        pos, vel, acc, jerk = correct(pos, vel, acc, jerk, spread[0:3], spread[3:6], stride, hit)
        clock = jnp.where(hit, now, clock)
    return (pos, vel, acc, jerk, jnp.stack(recorded))


def solution(mesh):
    in_specs = (
        P(None, ("blk", "grp")),
        P(None, ("blk", "grp")),
        P(None, ("blk", "grp")),
        P(None, ("blk", "grp")),
        P(("blk", "grp")),
        P(("blk", "grp")),
        P(None, ("blk", "grp")),
        P(None, ("blk", "grp")),
    )
    out_specs = (
        P(None, ("blk", "grp")),
        P(None, ("blk", "grp")),
        P(None, ("blk", "grp")),
        P(None, ("blk", "grp")),
        P(None, None, ("blk", "grp")),
    )
    return jax.shard_map(body, mesh=mesh, in_specs=in_specs, out_specs=out_specs, check_vma=False)
```

profile of v0, /device:TPU:8, one launch (start us, length us, event | category | flops | bytes accessed | tf_op | source)
XLA Modules:
  0.0 726.7 jit_solution(7980893641859117160)
XLA Ops:
  2.1 4.9 collective-permute-start
  7.0 1.3 fusion.138
  10.0 69.5 %all-gather = f32[64,24,6]{1,2,0:T(8,128)S(1)} all-gather(f32[1,24,6]{1,2,0:T(8,128)S(1)} %convolution_bitcast_fusion.1), channel_id=1, replica_groups=mesh['blk'=8,'grp'=64] {'grp'}, dimensions={0}, use_global_device_ids=true | all-gather | bytes 37440 | tf_op jit(solution)/shard_map/all_gather | solution.py:75
  79.8 3.7 while.160
  84.8 1.3 dynamic-slice
  86.8 5.0 collective-permute-start.1
  91.7 8.1 %while.161 = (s32[]{:T(128)}, f32[3,6,512]{2,1,0:T(8,128)S(1)}, f32[7,256]{1,0:T(8,128)}, f32[3,6,512]{2,1,0:T(8,128)S(1)}, s32[]{:T(128)}, /*index=5*/s32[]{:T(128)}, s32[]{}) while((s32[]{:T(128)}, f32[3,6,512]{2,1,0:T(8,128)S(1)}, f32[7,256]{1,0:T(8,128)}, f32[3,6,512]{2,1,0:T(8,128)S(1)}, s32[]{:T(128)}, /*index=5*/s32[]{:T(128)}, ...), condition=%wide.region_9.10_spmd, body=%wide.region_6.9_spmd.sunk | while | flops 6160387 | bytes 8510565 | solution.py:51
  94.4 0.8 fusion.187
  97.1 0.8 fusion.187
  99.8 3.4 collective-permute-start.2
  103.2 8.1 %while.162 = (s32[]{:T(128)}, f32[3,6,512]{2,1,0:T(8,128)S(1)}, f32[7,256]{1,0:T(8,128)}, f32[3,6,512]{2,1,0:T(8,128)S(1)}, s32[]{:T(128)}, /*index=5*/s32[]{:T(128)}, s32[]{}) while((s32[]{:T(128)}, f32[3,6,512]{2,1,0:T(8,128)S(1)}, f32[7,256]{1,0:T(8,128)}, f32[3,6,512]{2,1,0:T(8,128)S(1)}, s32[]{:T(128)}, /*index=5*/s32[]{:T(128)}, ...), condition=%wide.region_13.14_spmd, body=%wide.region_10.13_spmd.sunk | while | flops 6160387 | bytes 8510565 | solution.py:51
  103.3 0.8 fusion.190
  106.0 0.8 fusion.190
  108.7 0.8 fusion.190
  111.4 4.7 collective-permute-start.3
  116.1 8.1 %while.163 = (s32[]{:T(128)}, f32[3,6,512]{2,1,0:T(8,128)S(1)}, f32[7,256]{1,0:T(8,128)}, f32[3,6,512]{2,1,0:T(8,128)S(1)}, s32[]{:T(128)}, /*index=5*/s32[]{:T(128)}, s32[]{}) while((s32[]{:T(128)}, f32[3,6,512]{2,1,0:T(8,128)S(1)}, f32[7,256]{1,0:T(8,128)}, f32[3,6,512]{2,1,0:T(8,128)S(1)}, s32[]{:T(128)}, /*index=5*/s32[]{:T(128)}, ...), condition=%wide.region_17.18_spmd, body=%wide.region_14.17_spmd.sunk | while | flops 6160387 | bytes 8510565 | solution.py:51
  116.1 0.8 fusion.193
  118.8 0.8 fusion.193
  121.5 0.8 fusion.193
  124.2 3.4 collective-permute-start.4
  127.6 8.1 %while.164 = (s32[]{:T(128)}, f32[3,6,512]{2,1,0:T(8,128)S(1)}, f32[7,256]{1,0:T(8,128)}, f32[3,6,512]{2,1,0:T(8,128)S(1)}, s32[]{:T(128)}, /*index=5*/s32[]{:T(128)}, s32[]{}) while((s32[]{:T(128)}, f32[3,6,512]{2,1,0:T(8,128)S(1)}, f32[7,256]{1,0:T(8,128)}, f32[3,6,512]{2,1,0:T(8,128)S(1)}, s32[]{:T(128)}, /*index=5*/s32[]{:T(128)}, ...), condition=%wide.region_21.22_spmd, body=%wide.region_18.21_spmd.sunk | while | flops 6160387 | bytes 8510565 | solution.py:51
  127.6 0.8 fusion.196
  130.3 0.8 fusion.196
  133.0 0.8 fusion.196
  135.7 3.6 collective-permute-start.5
  139.4 8.1 %while.165 = (s32[]{:T(128)}, f32[3,6,512]{2,1,0:T(8,128)S(1)}, f32[7,256]{1,0:T(8,128)}, f32[3,6,512]{2,1,0:T(8,128)S(1)}, s32[]{:T(128)}, /*index=5*/s32[]{:T(128)}, s32[]{}) while((s32[]{:T(128)}, f32[3,6,512]{2,1,0:T(8,128)S(1)}, f32[7,256]{1,0:T(8,128)}, f32[3,6,512]{2,1,0:T(8,128)S(1)}, s32[]{:T(128)}, /*index=5*/s32[]{:T(128)}, ...), condition=%wide.region_25.26_spmd, body=%wide.region_22.25_spmd.sunk | while | flops 6160387 | bytes 8510565 | solution.py:51
  139.4 0.8 fusion.199
  142.1 0.8 fusion.199
  144.8 0.8 fusion.199
  147.5 3.4 collective-permute-start.6
  150.9 8.1 %while.166 = (s32[]{:T(128)}, f32[3,6,512]{2,1,0:T(8,128)S(1)}, f32[7,256]{1,0:T(8,128)}, f32[3,6,512]{2,1,0:T(8,128)S(1)}, s32[]{:T(128)}, /*index=5*/s32[]{:T(128)}, s32[]{}) while((s32[]{:T(128)}, f32[3,6,512]{2,1,0:T(8,128)S(1)}, f32[7,256]{1,0:T(8,128)}, f32[3,6,512]{2,1,0:T(8,128)S(1)}, s32[]{:T(128)}, /*index=5*/s32[]{:T(128)}, ...), condition=%wide.region_29.30_spmd, body=%wide.region_26.29_spmd.sunk | while | flops 6160387 | bytes 8510565 | solution.py:51
  153.6 0.8 fusion.202
  156.3 0.8 fusion.202
  159.0 3.7 while.167
  162.8 207.4 %all-reduce = f32[6,1536]{1,0:T(8,128)S(1)} all-reduce(f32[6,1536]{1,0:T(8,128)S(1)} %bitcast.364), channel_id=2, replica_groups=mesh['blk'=8,'grp'=64] {'grp'}, use_global_device_ids=true, to_apply=%region_34.35.clone | all-reduce | flops 9216 | bytes 73728
  370.7 60.2 %all-gather.1 = f32[64,24,6]{1,2,0:T(8,128)S(1)} all-gather(f32[1,24,6]{1,2,0:T(8,128)S(1)} %convolution_bitcast_fusion), channel_id=1, replica_groups=mesh['blk'=8,'grp'=64] {'grp'}, dimensions={0}, use_global_device_ids=true | all-gather | bytes 37440 | tf_op jit(solution)/shard_map/all_gather | solution.py:75
  431.1 5.0 collective-permute-start.7
  436.1 3.7 while.168
  439.9 3.4 collective-permute-start.8
  443.3 8.1 %while.169 = (s32[]{:T(128)}, f32[3,6,512]{2,1,0:T(8,128)S(1)}, f32[7,256]{1,0:T(8,128)}, f32[3,6,512]{2,1,0:T(8,128)S(1)}, s32[]{:T(128)}, /*index=5*/s32[]{:T(128)}, s32[]{}) while((s32[]{:T(128)}, f32[3,6,512]{2,1,0:T(8,128)S(1)}, f32[7,256]{1,0:T(8,128)}, f32[3,6,512]{2,1,0:T(8,128)S(1)}, s32[]{:T(128)}, /*index=5*/s32[]{:T(128)}, ...), condition=%wide.region_42.43_spmd, body=%wide.region_39.42_spmd.sunk | while | flops 6160387 | bytes 8510565 | solution.py:51
  443.3 0.8 fusion.210
  446.0 0.8 fusion.210
  448.7 0.8 fusion.210
  451.4 5.0 collective-permute-start.9
  456.4 8.1 %while.170 = (s32[]{:T(128)}, f32[3,6,512]{2,1,0:T(8,128)S(1)}, f32[7,256]{1,0:T(8,128)}, f32[3,6,512]{2,1,0:T(8,128)S(1)}, s32[]{:T(128)}, /*index=5*/s32[]{:T(128)}, s32[]{}) while((s32[]{:T(128)}, f32[3,6,512]{2,1,0:T(8,128)S(1)}, f32[7,256]{1,0:T(8,128)}, f32[3,6,512]{2,1,0:T(8,128)S(1)}, s32[]{:T(128)}, /*index=5*/s32[]{:T(128)}, ...), condition=%wide.region_46.47_spmd, body=%wide.region_43.46_spmd.sunk | while | flops 6160387 | bytes 8510565 | solution.py:51
  456.4 0.8 fusion.213
  459.1 0.8 fusion.213
  461.8 0.8 fusion.213
  464.5 3.4 collective-permute-start.10
  467.9 8.1 %while.171 = (s32[]{:T(128)}, f32[3,6,512]{2,1,0:T(8,128)S(1)}, f32[7,256]{1,0:T(8,128)}, f32[3,6,512]{2,1,0:T(8,128)S(1)}, s32[]{:T(128)}, /*index=5*/s32[]{:T(128)}, s32[]{}) while((s32[]{:T(128)}, f32[3,6,512]{2,1,0:T(8,128)S(1)}, f32[7,256]{1,0:T(8,128)}, f32[3,6,512]{2,1,0:T(8,128)S(1)}, s32[]{:T(128)}, /*index=5*/s32[]{:T(128)}, ...), condition=%wide.region_50.51_spmd, body=%wide.region_47.50_spmd.sunk | while | flops 6160387 | bytes 8510565 | solution.py:51
  468.0 0.8 fusion.216
  470.7 0.8 fusion.216
  473.4 0.8 fusion.216
  476.1 4.7 collective-permute-start.11
  480.8 8.1 %while.172 = (s32[]{:T(128)}, f32[3,6,512]{2,1,0:T(8,128)S(1)}, f32[7,256]{1,0:T(8,128)}, f32[3,6,512]{2,1,0:T(8,128)S(1)}, s32[]{:T(128)}, /*index=5*/s32[]{:T(128)}, s32[]{}) while((s32[]{:T(128)}, f32[3,6,512]{2,1,0:T(8,128)S(1)}, f32[7,256]{1,0:T(8,128)}, f32[3,6,512]{2,1,0:T(8,128)S(1)}, s32[]{:T(128)}, /*index=5*/s32[]{:T(128)}, ...), condition=%wide.region_54.55_spmd, body=%wide.region_51.54_spmd.sunk | while | flops 6160387 | bytes 8510565 | solution.py:51
  480.8 0.8 fusion.219
  483.5 0.8 fusion.219
  486.2 0.8 fusion.219
  488.9 3.4 collective-permute-start.12
  492.3 8.1 %while.173 = (s32[]{:T(128)}, f32[3,6,512]{2,1,0:T(8,128)S(1)}, f32[7,256]{1,0:T(8,128)}, f32[3,6,512]{2,1,0:T(8,128)S(1)}, s32[]{:T(128)}, /*index=5*/s32[]{:T(128)}, s32[]{}) while((s32[]{:T(128)}, f32[3,6,512]{2,1,0:T(8,128)S(1)}, f32[7,256]{1,0:T(8,128)}, f32[3,6,512]{2,1,0:T(8,128)S(1)}, s32[]{:T(128)}, /*index=5*/s32[]{:T(128)}, ...), condition=%wide.region_58.59_spmd, body=%wide.region_55.58_spmd.sunk | while | flops 6160387 | bytes 8510565 | solution.py:51
  500.4 5.5 collective-permute-start.13
  505.9 8.1 %while.174 = (s32[]{:T(128)}, f32[3,6,512]{2,1,0:T(8,128)S(1)}, f32[7,256]{1,0:T(8,128)}, f32[3,6,512]{2,1,0:T(8,128)S(1)}, s32[]{:T(128)}, /*index=5*/s32[]{:T(128)}, s32[]{}) while((s32[]{:T(128)}, f32[3,6,512]{2,1,0:T(8,128)S(1)}, f32[7,256]{1,0:T(8,128)}, f32[3,6,512]{2,1,0:T(8,128)S(1)}, s32[]{:T(128)}, /*index=5*/s32[]{:T(128)}, ...), condition=%wide.region_62.63_spmd, body=%wide.region_59.62_spmd.sunk | while | flops 6160387 | bytes 8510565 | solution.py:51
  514.0 3.7 while.175
  517.8 207.4 %all-reduce.1 = f32[6,1536]{1,0:T(8,128)S(1)} all-reduce(f32[6,1536]{1,0:T(8,128)S(1)} %bitcast.365), channel_id=3, replica_groups=mesh['blk'=8,'grp'=64] {'grp'}, use_global_device_ids=true, to_apply=%region_67.68.clone | all-reduce | flops 9216 | bytes 73728
  (371 shorter events, 95.3 us)
Async XLA Ops:
  2.1 84.7 %collective-permute-start = (f32[7,256]{1,0:T(8,128)S(1)}, f32[7,256]{1,0:T(8,128)}, u32[]{:S(2)}, u32[]{:S(2)}) collective-permute-start(f32[7,256]{1,0:T(8,128)S(1)} %pad_maximum_fusion.1), channel_id=1, source_target_pairs={{0,64},{64,128},{128,192},{192,256},{256,320},{320,384},{384,448},... | collective-permute-start | bytes 21512 | tf_op jit(solution)/shard_map/ppermute | solution.py:13
  79.8 3.7 copy-start.4
  86.8 13.1 %collective-permute-start.1 = (f32[7,256]{1,0:T(8,128)}, f32[7,256]{1,0:T(8,128)}, u32[]{:S(2)}, u32[]{:S(2)}) collective-permute-start(f32[7,256]{1,0:T(8,128)} %collective-permute-done), channel_id=1, source_target_pairs={{0,64},{64,128},{128,192},{192,256},{256,320},{320,384},{384,448},... | collective-permute-start | bytes 21512 | tf_op jit(solution)/shard_map/ppermute | solution.py:13
  99.8 11.5 %collective-permute-start.2 = (f32[7,256]{1,0:T(8,128)}, f32[7,256]{1,0:T(8,128)}, u32[]{:S(2)}, u32[]{:S(2)}) collective-permute-start(f32[7,256]{1,0:T(8,128)} %collective-permute-done.1), channel_id=1, source_target_pairs={{0,64},{64,128},{128,192},{192,256},{256,320},{320,384},{384,448},... | collective-permute-start | bytes 21512 | tf_op jit(solution)/shard_map/ppermute | solution.py:13
  111.4 12.8 %collective-permute-start.3 = (f32[7,256]{1,0:T(8,128)}, f32[7,256]{1,0:T(8,128)}, u32[]{:S(2)}, u32[]{:S(2)}) collective-permute-start(f32[7,256]{1,0:T(8,128)} %collective-permute-done.2), channel_id=1, source_target_pairs={{0,64},{64,128},{128,192},{192,256},{256,320},{320,384},{384,448},... | collective-permute-start | bytes 21512 | tf_op jit(solution)/shard_map/ppermute | solution.py:13
  124.2 11.5 %collective-permute-start.4 = (f32[7,256]{1,0:T(8,128)}, f32[7,256]{1,0:T(8,128)}, u32[]{:S(2)}, u32[]{:S(2)}) collective-permute-start(f32[7,256]{1,0:T(8,128)} %collective-permute-done.3), channel_id=1, source_target_pairs={{0,64},{64,128},{128,192},{192,256},{256,320},{320,384},{384,448},... | collective-permute-start | bytes 21512 | tf_op jit(solution)/shard_map/ppermute | solution.py:13
  135.7 11.8 %collective-permute-start.5 = (f32[7,256]{1,0:T(8,128)}, f32[7,256]{1,0:T(8,128)}, u32[]{:S(2)}, u32[]{:S(2)}) collective-permute-start(f32[7,256]{1,0:T(8,128)} %collective-permute-done.4), channel_id=1, source_target_pairs={{0,64},{64,128},{128,192},{192,256},{256,320},{320,384},{384,448},... | collective-permute-start | bytes 21512 | tf_op jit(solution)/shard_map/ppermute | solution.py:13
  147.5 11.5 %collective-permute-start.6 = (f32[7,256]{1,0:T(8,128)}, f32[7,256]{1,0:T(8,128)S(1)}, u32[]{:S(2)}, u32[]{:S(2)}) collective-permute-start(f32[7,256]{1,0:T(8,128)} %collective-permute-done.5), channel_id=1, source_target_pairs={{0,64},{64,128},{128,192},{192,256},{256,320},{320,384},{384,448},... | collective-permute-start | bytes 21512 | tf_op jit(solution)/shard_map/ppermute | solution.py:13
  159.0 211.4 %copy-start = (f32[3,256]{1,0:T(4,128)S(1)}, f32[3,256]{1,0:T(4,128)}, u32[]{:S(2)}) copy-start(f32[3,256]{1,0:T(4,128)} %param.43) | copy-start | bytes 9220
  159.0 211.4 %copy-start.1 = (f32[3,256]{1,0:T(4,128)S(1)}, f32[3,256]{1,0:T(4,128)}, u32[]{:S(2)}) copy-start(f32[3,256]{1,0:T(4,128)} %param.40) | copy-start | bytes 9220
  159.0 211.4 %copy-start.2 = (f32[3,256]{1,0:T(4,128)S(1)}, f32[3,256]{1,0:T(4,128)}, u32[]{:S(2)}) copy-start(f32[3,256]{1,0:T(4,128)} %param.41) | copy-start | bytes 9220
  159.0 211.4 %copy-start.3 = (f32[3,256]{1,0:T(4,128)S(1)}, f32[3,256]{1,0:T(4,128)}, u32[]{:S(2)}) copy-start(f32[3,256]{1,0:T(4,128)} %param.42) | copy-start | bytes 9220
  431.1 8.8 %collective-permute-start.7 = (f32[7,256]{1,0:T(8,128)S(1)}, f32[7,256]{1,0:T(8,128)}, u32[]{:S(2)}, u32[]{:S(2)}) collective-permute-start(f32[7,256]{1,0:T(8,128)S(1)} %pad_maximum_fusion), channel_id=1, source_target_pairs={{0,64},{64,128},{128,192},{192,256},{256,320},{320,384},{384,448},... | collective-permute-start | bytes 21512 | tf_op jit(solution)/shard_map/ppermute | solution.py:13
  439.9 11.5 %collective-permute-start.8 = (f32[7,256]{1,0:T(8,128)}, f32[7,256]{1,0:T(8,128)}, u32[]{:S(2)}, u32[]{:S(2)}) collective-permute-start(f32[7,256]{1,0:T(8,128)} %collective-permute-done.7), channel_id=1, source_target_pairs={{0,64},{64,128},{128,192},{192,256},{256,320},{320,384},{384,448},... | collective-permute-start | bytes 21512 | tf_op jit(solution)/shard_map/ppermute | solution.py:13
  451.4 13.1 %collective-permute-start.9 = (f32[7,256]{1,0:T(8,128)}, f32[7,256]{1,0:T(8,128)}, u32[]{:S(2)}, u32[]{:S(2)}) collective-permute-start(f32[7,256]{1,0:T(8,128)} %collective-permute-done.8), channel_id=1, source_target_pairs={{0,64},{64,128},{128,192},{192,256},{256,320},{320,384},{384,448},... | collective-permute-start | bytes 21512 | tf_op jit(solution)/shard_map/ppermute | solution.py:13
  464.5 11.5 %collective-permute-start.10 = (f32[7,256]{1,0:T(8,128)}, f32[7,256]{1,0:T(8,128)}, u32[]{:S(2)}, u32[]{:S(2)}) collective-permute-start(f32[7,256]{1,0:T(8,128)} %collective-permute-done.9), channel_id=1, source_target_pairs={{0,64},{64,128},{128,192},{192,256},{256,320},{320,384},{384,448},... | collective-permute-start | bytes 21512 | tf_op jit(solution)/shard_map/ppermute | solution.py:13
  476.1 12.8 %collective-permute-start.11 = (f32[7,256]{1,0:T(8,128)}, f32[7,256]{1,0:T(8,128)}, u32[]{:S(2)}, u32[]{:S(2)}) collective-permute-start(f32[7,256]{1,0:T(8,128)} %collective-permute-done.10), channel_id=1, source_target_pairs={{0,64},{64,128},{128,192},{192,256},{256,320},{320,384},{384,448},... | collective-permute-start | bytes 21512 | tf_op jit(solution)/shard_map/ppermute | solution.py:13
  488.9 11.5 %collective-permute-start.12 = (f32[7,256]{1,0:T(8,128)}, f32[7,256]{1,0:T(8,128)}, u32[]{:S(2)}, u32[]{:S(2)}) collective-permute-start(f32[7,256]{1,0:T(8,128)} %collective-permute-done.11), channel_id=1, source_target_pairs={{0,64},{64,128},{128,192},{192,256},{256,320},{320,384},{384,448},... | collective-permute-start | bytes 21512 | tf_op jit(solution)/shard_map/ppermute | solution.py:13
  500.4 13.6 %collective-permute-start.13 = (f32[7,256]{1,0:T(8,128)}, f32[7,256]{1,0:T(8,128)S(1)}, u32[]{:S(2)}, u32[]{:S(2)}) collective-permute-start(f32[7,256]{1,0:T(8,128)} %collective-permute-done.12), channel_id=1, source_target_pairs={{0,64},{64,128},{128,192},{192,256},{256,320},{320,384},{384,448},... | collective-permute-start | bytes 21512 | tf_op jit(solution)/shard_map/ppermute | solution.py:13
  514.0 212.1 %copy-start.5 = (pred[256]{0:T(512)(128)(4,1)S(1)}, pred[256]{0:T(512)(128)(4,1)}, u32[]{:S(2)}) copy-start(pred[256]{0:T(512)(128)(4,1)} %broadcast_compare_fusion.1) | copy-start | bytes 772
where the time goes:
time: 733 us; the launch traced here: 727 us
  blocking collectives  544 us (74%)
  other arithmetic  60.6 us (8%)
  starting transfers between devices  58.6 us (8%)
  local copies, waits for them, and re-layouts  58.3 us (8%)
    unnamed x2, blocking collectives  415 us
    all_gather x2, blocking collectives, body(): row_actives = lax.all_gather(chosen, 'grp', axis=1, tiled=True)  130 us
    ppermute x14, starting transfers between devices, passed_along(): return lax.ppermute(value, axis, pairs)  58.6 us
    slice x42, local copies, waits for them, and re-layouts, block_terms(): dvel = jpart[3:6, :, None] - iblock[3:6, None, :]  27.9 us
    reduce_sum x48, other arithmetic, block_terms(): accel = jnp.sum(weight[None] * dpos, axis=1)  27.4 us
    slice x42, local copies, waits for them, and re-layouts, block_terms(): weight = jpart[6][:, None] * inverse * inverse * inverse  25.3 us
    mul x48, other arithmetic, block_terms(): jerk = jnp.sum(weight[None] * (dvel - radial[None] * dpos), axis=1)  15.3 us
  transfers between devices with their start and end apart: 14, of which 0 were waited for; matrix products, arithmetic and copies ran while one was open for 15% of the time, Pallas kernels for 0%

commit v1 on v0

--- a/solution.py
+++ b/solution.py
@@ -5,6 +5,13 @@
 
 STEP_BASE = 0.125
 SOFTEN = 0.01
+
+
+def swapped_in(x, mesh_axis, dim):
+    n_dev = lax.axis_size(mesh_axis)
+    parts = jnp.stack([x for _ in range(n_dev)])
+    parts = lax.all_to_all(parts, mesh_axis, split_axis=0, concat_axis=0)
+    return jnp.concatenate(parts, axis=dim)
 
 
 def passed_along(value, axis, steps):
@@ -72,7 +79,7 @@
         pred_both = jnp.concatenate([pred_pos, pred_vel], axis=0)
         chosen = jnp.dot(pred_both, picker.T, precision=lax.Precision.HIGHEST)
         jdata = jnp.concatenate([pred_pos, pred_vel, mass[None, :]], axis=0)
-        row_actives = lax.all_gather(chosen, "grp", axis=1, tiled=True)
+        row_actives = swapped_in(chosen, "grp", 1)
         travel = jdata
         partial_value = pair_terms(row_actives, travel)
         for turn in range(loop_len - 1):

time: 733 us -> 628 us (0.86)
  the two profiles are of different devices: /device:TPU:8 before, /device:TPU:28 now
where the time goes in v1:
time: 628 us; the launch traced here: 626 us
  blocking collectives  416 us (66%)
  starting transfers between devices  99.7 us (16%)
  other arithmetic  62.3 us (10%)
  waiting for transfers between devices  26.4 us (4%)
  local copies, waits for them, and re-layouts  16.7 us (3%)
    unnamed x2, blocking collectives  416 us
    ppermute x14, starting transfers between devices, passed_along(): return lax.ppermute(value, axis, pairs)  75.3 us
    reduce_sum x48, other arithmetic, block_terms(): accel = jnp.sum(weight[None] * dpos, axis=1)  27.4 us
    all_to_all x2, starting transfers between devices, swapped_in(): parts = lax.all_to_all(parts, mesh_axis, split_axis=0, concat_axis=0)  24.4 us
    ppermute x14, waiting for transfers between devices, passed_along(): return lax.ppermute(value, axis, pairs)  23.3 us
    mul x48, other arithmetic, block_terms(): jerk = jnp.sum(weight[None] * (dvel - radial[None] * dpos), axis=1)  15.2 us
    sub x48, other arithmetic, block_terms(): dvel = jpart[3:6, :, None] - iblock[3:6, None, :]  12.9 us
  transfers between devices with their start and end apart: 16, of which 9 were waited for; matrix products, arithmetic and copies ran while one was open for 8% of the time, Pallas kernels for 0%

profile of v1, /device:TPU:28, one launch (start us, length us, event | category | flops | bytes accessed | tf_op | source)
XLA Modules:
  0.0 626.3 jit_solution(12382770390779178479)
XLA Ops:
  1.3 0.7 multiply_add_fusion.5
  2.1 7.4 %collective-permute-start = (f32[7,256]{1,0:T(8,128)S(1)}, f32[7,256]{1,0:T(8,128)S(1)}, u32[]{:S(2)}, u32[]{:S(2)}) collective-permute-start(f32[7,256]{1,0:T(8,128)S(1)} %pad_maximum_fusion.1), channel_id=1, source_target_pairs={{0,64},{64,128},{128,192},{192,256},{256,320},{320,384},{384,448},... | collective-permute-start | bytes 21512 | tf_op jit(solution)/shard_map/ppermute | solution.py:20
  9.5 0.8 slice_bitcast_fusion.1
  10.3 1.3 fusion.140
  11.6 7.1 %collective-permute-start.1 = (f32[7,256]{1,0:T(8,128)S(1)}, f32[7,256]{1,0:T(8,128)S(1)}, u32[]{:S(2)}, u32[]{:S(2)}) collective-permute-start(f32[7,256]{1,0:T(8,128)S(1)} %collective-permute-done), channel_id=1, source_target_pairs={{0,64},{64,128},{128,192},{192,256},{256,320},{320,384},{384,448},... | collective-permute-start | bytes 21512 | tf_op jit(solution)/shard_map/ppermute | solution.py:20
  19.3 0.7 collective-permute-done.1
  20.0 7.8 %collective-permute-start.2 = (f32[7,256]{1,0:T(8,128)S(1)}, f32[7,256]{1,0:T(8,128)S(1)}, u32[]{:S(2)}, u32[]{:S(2)}) collective-permute-start(f32[7,256]{1,0:T(8,128)S(1)} %collective-permute-done.1), channel_id=1, source_target_pairs={{0,64},{64,128},{128,192},{192,256},{256,320},{320,384},{384,448},... | collective-permute-start | bytes 21512 | tf_op jit(solution)/shard_map/ppermute | solution.py:20
  28.1 0.8 reshape.339
  28.9 12.3 %all-to-all-start = ((f32[64,1,144]{2,1,0:T(1,128)}), f32[64,1,144]{2,1,0:T(1,128)S(1)}, u32[]{:S(2)}, u32[]{:S(2)}) async-start(f32[64,1,144]{2,1,0:T(1,128)} %reshape.339), calls=%async_computation | async-start | bytes 131072 | tf_op jit(solution)/shard_map/all_to_all | solution.py:13
  41.1 1.9 collective-permute-start.3
  43.1 0.7 convert_multiply_fusion
  43.8 4.4 collective-permute-done.3
  48.2 4.0 collective-permute-start.4
  52.3 2.9 collective-permute-done.4
  55.2 6.1 collective-permute-start.5
  61.4 1.3 dynamic-slice
  63.3 7.3 %collective-permute-start.6 = (f32[7,256]{1,0:T(8,128)}, f32[7,256]{1,0:T(8,128)S(1)}, u32[]{:S(2)}, u32[]{:S(2)}) collective-permute-start(f32[7,256]{1,0:T(8,128)} %collective-permute-done.5), channel_id=1, source_target_pairs={{0,64},{64,128},{128,192},{192,256},{256,320},{320,384},{384,448},... | collective-permute-start | bytes 21512 | tf_op jit(solution)/shard_map/ppermute | solution.py:20
  71.1 0.8 reduce
  72.3 8.1 %while.166 = (s32[]{:T(128)}, f32[3,6,512]{2,1,0:T(8,128)S(1)}, f32[7,256]{1,0:T(8,128)}, f32[3,6,512]{2,1,0:T(8,128)S(1)}, s32[]{:T(128)}, /*index=5*/s32[]{:T(128)}, s32[]{}) while((s32[]{:T(128)}, f32[3,6,512]{2,1,0:T(8,128)S(1)}, f32[7,256]{1,0:T(8,128)}, f32[3,6,512]{2,1,0:T(8,128)S(1)}, s32[]{:T(128)}, /*index=5*/s32[]{:T(128)}, ...), condition=%wide.region_29.30_spmd, body=%wide.region_26.29_spmd.sunk | while | flops 6160387 | bytes 8510565 | solution.py:58
  72.3 0.8 fusion.204
  73.4 0.7 slice.1395
  75.0 0.8 fusion.204
  76.1 0.7 slice.1395
  77.7 0.8 fusion.204
  78.8 0.7 slice.1395
  80.4 3.7 while.167
  84.2 3.8 while.165
  88.0 3.8 while.164
  91.8 3.8 while.163
  95.5 3.8 while.162
  99.3 3.8 while.161
  103.1 3.7 while.160
  106.8 208.1 %all-reduce = f32[6,1536]{1,0:T(8,128)S(1)} all-reduce(f32[6,1536]{1,0:T(8,128)S(1)} %bitcast.358), channel_id=2, replica_groups=mesh['blk'=8,'grp'=64] {'grp'}, use_global_device_ids=true, to_apply=%region_34.35.clone | all-reduce | flops 9216 | bytes 73728
  315.3 1.9 collective-permute-start.7
  317.2 5.1 collective-permute-done.7
  322.3 4.0 collective-permute-start.8
  327.0 2.4 collective-permute-done.8
  329.4 6.1 collective-permute-start.9
  335.6 1.3 collective-permute-done.9
  336.8 7.8 %collective-permute-start.10 = (f32[7,256]{1,0:T(8,128)S(1)}, f32[7,256]{1,0:T(8,128)S(1)}, u32[]{:S(2)}, u32[]{:S(2)}) collective-permute-start(f32[7,256]{1,0:T(8,128)S(1)} %collective-permute-done.9), channel_id=1, source_target_pairs={{0,64},{64,128},{128,192},{192,256},{256,320},{320,384},{384,448},... | collective-permute-start | bytes 21512 | tf_op jit(solution)/shard_map/ppermute | solution.py:20
  344.7 1.3 collective-permute-done.10
  346.0 7.8 %collective-permute-start.11 = (f32[7,256]{1,0:T(8,128)S(1)}, f32[7,256]{1,0:T(8,128)S(1)}, u32[]{:S(2)}, u32[]{:S(2)}) collective-permute-start(f32[7,256]{1,0:T(8,128)S(1)} %collective-permute-done.10), channel_id=1, source_target_pairs={{0,64},{64,128},{128,192},{192,256},{256,320},{320,384},{384,448},... | collective-permute-start | bytes 21512 | tf_op jit(solution)/shard_map/ppermute | solution.py:20
  354.0 0.8 reshape.341
  354.8 12.2 %all-to-all-start.1 = ((f32[64,1,144]{2,1,0:T(1,128)}), f32[64,1,144]{2,1,0:T(1,128)S(1)}, u32[]{:S(2)}, u32[]{:S(2)}) async-start(f32[64,1,144]{2,1,0:T(1,128)} %reshape.341), calls=%async_computation.1 | async-start | bytes 131072 | tf_op jit(solution)/shard_map/all_to_all | solution.py:13
  367.0 1.9 collective-permute-start.12
  369.0 5.1 collective-permute-done.12
  374.2 4.0 collective-permute-start.13
  378.2 3.2 all-to-all-done.1
  381.4 0.8 reduce.1
  382.6 3.8 while.169
  386.3 3.8 while.170
  390.1 3.8 while.171
  393.9 3.8 while.172
  397.6 3.8 while.173
  401.4 8.1 %while.174 = (s32[]{:T(128)}, f32[3,6,512]{2,1,0:T(8,128)S(1)}, f32[7,256]{1,0:T(8,128)}, f32[3,6,512]{2,1,0:T(8,128)S(1)}, s32[]{:T(128)}, /*index=5*/s32[]{:T(128)}, s32[]{}) while((s32[]{:T(128)}, f32[3,6,512]{2,1,0:T(8,128)S(1)}, f32[7,256]{1,0:T(8,128)}, f32[3,6,512]{2,1,0:T(8,128)S(1)}, s32[]{:T(128)}, /*index=5*/s32[]{:T(128)}, ...), condition=%wide.region_62.63_spmd, body=%wide.region_59.62_spmd.sunk | while | flops 6160387 | bytes 8510565 | solution.py:58
  401.5 0.8 fusion.227
  402.5 0.7 slice.1464
  404.2 0.8 fusion.227
  405.2 0.7 slice.1464
  406.9 0.8 fusion.227
  407.9 0.7 slice.1464
  409.6 3.7 while.168
  413.3 3.7 while.175
  417.1 207.8 %all-reduce.1 = f32[6,1536]{1,0:T(8,128)S(1)} all-reduce(f32[6,1536]{1,0:T(8,128)S(1)} %bitcast.359), channel_id=3, replica_groups=mesh['blk'=8,'grp'=64] {'grp'}, use_global_device_ids=true, to_apply=%region_67.68.clone | all-reduce | flops 9216 | bytes 73728
  (376 shorter events, 62.9 us)
Async XLA Ops:
  2.1 9.5 %collective-permute-start = (f32[7,256]{1,0:T(8,128)S(1)}, f32[7,256]{1,0:T(8,128)S(1)}, u32[]{:S(2)}, u32[]{:S(2)}) collective-permute-start(f32[7,256]{1,0:T(8,128)S(1)} %pad_maximum_fusion.1), channel_id=1, source_target_pairs={{0,64},{64,128},{128,192},{192,256},{256,320},{320,384},{384,448},... | collective-permute-start | bytes 21512 | tf_op jit(solution)/shard_map/ppermute | solution.py:20
  11.6 8.4 %collective-permute-start.1 = (f32[7,256]{1,0:T(8,128)S(1)}, f32[7,256]{1,0:T(8,128)S(1)}, u32[]{:S(2)}, u32[]{:S(2)}) collective-permute-start(f32[7,256]{1,0:T(8,128)S(1)} %collective-permute-done), channel_id=1, source_target_pairs={{0,64},{64,128},{128,192},{192,256},{256,320},{320,384},{384,448},... | collective-permute-start | bytes 21512 | tf_op jit(solution)/shard_map/ppermute | solution.py:20
  20.0 21.1 %collective-permute-start.2 = (f32[7,256]{1,0:T(8,128)S(1)}, f32[7,256]{1,0:T(8,128)S(1)}, u32[]{:S(2)}, u32[]{:S(2)}) collective-permute-start(f32[7,256]{1,0:T(8,128)S(1)} %collective-permute-done.1), channel_id=1, source_target_pairs={{0,64},{64,128},{128,192},{192,256},{256,320},{320,384},{384,448},... | collective-permute-start | bytes 21512 | tf_op jit(solution)/shard_map/ppermute | solution.py:20
  28.9 41.8 %all-to-all-start = ((f32[64,1,144]{2,1,0:T(1,128)}), f32[64,1,144]{2,1,0:T(1,128)S(1)}, u32[]{:S(2)}, u32[]{:S(2)}) async-start(f32[64,1,144]{2,1,0:T(1,128)} %reshape.339), calls=%async_computation | async-start | bytes 131072 | tf_op jit(solution)/shard_map/all_to_all | solution.py:13
  41.1 7.0 %collective-permute-start.3 = (f32[7,256]{1,0:T(8,128)S(1)}, f32[7,256]{1,0:T(8,128)S(1)}, u32[]{:S(2)}, u32[]{:S(2)}) collective-permute-start(f32[7,256]{1,0:T(8,128)S(1)} %collective-permute-done.2), channel_id=1, source_target_pairs={{0,64},{64,128},{128,192},{192,256},{256,320},{320,384},{384,448},... | collective-permute-start | bytes 21512 | tf_op jit(solution)/shard_map/ppermute | solution.py:20
  48.2 7.0 %collective-permute-start.4 = (f32[7,256]{1,0:T(8,128)S(1)}, f32[7,256]{1,0:T(8,128)S(1)}, u32[]{:S(2)}, u32[]{:S(2)}) collective-permute-start(f32[7,256]{1,0:T(8,128)S(1)} %collective-permute-done.3), channel_id=1, source_target_pairs={{0,64},{64,128},{128,192},{192,256},{256,320},{320,384},{384,448},... | collective-permute-start | bytes 21512 | tf_op jit(solution)/shard_map/ppermute | solution.py:20
  55.2 8.1 %collective-permute-start.5 = (f32[7,256]{1,0:T(8,128)S(1)}, f32[7,256]{1,0:T(8,128)}, u32[]{:S(2)}, u32[]{:S(2)}) collective-permute-start(f32[7,256]{1,0:T(8,128)S(1)} %collective-permute-done.4), channel_id=1, source_target_pairs={{0,64},{64,128},{128,192},{192,256},{256,320},{320,384},{384,448},... | collective-permute-start | bytes 21512 | tf_op jit(solution)/shard_map/ppermute | solution.py:20
  63.3 17.1 %collective-permute-start.6 = (f32[7,256]{1,0:T(8,128)}, f32[7,256]{1,0:T(8,128)S(1)}, u32[]{:S(2)}, u32[]{:S(2)}) collective-permute-start(f32[7,256]{1,0:T(8,128)} %collective-permute-done.5), channel_id=1, source_target_pairs={{0,64},{64,128},{128,192},{192,256},{256,320},{320,384},{384,448},... | collective-permute-start | bytes 21512 | tf_op jit(solution)/shard_map/ppermute | solution.py:20
  103.1 212.1 %copy-start = (f32[3,256]{1,0:T(4,128)S(1)}, f32[3,256]{1,0:T(4,128)}, u32[]{:S(2)}) copy-start(f32[3,256]{1,0:T(4,128)} %param.43) | copy-start | bytes 9220
  103.1 212.1 %copy-start.1 = (f32[3,256]{1,0:T(4,128)S(1)}, f32[3,256]{1,0:T(4,128)}, u32[]{:S(2)}) copy-start(f32[3,256]{1,0:T(4,128)} %param.40) | copy-start | bytes 9220
  103.1 212.1 %copy-start.2 = (f32[3,256]{1,0:T(4,128)S(1)}, f32[3,256]{1,0:T(4,128)}, u32[]{:S(2)}) copy-start(f32[3,256]{1,0:T(4,128)} %param.41) | copy-start | bytes 9220
  103.1 212.1 %copy-start.3 = (f32[3,256]{1,0:T(4,128)S(1)}, f32[3,256]{1,0:T(4,128)}, u32[]{:S(2)}) copy-start(f32[3,256]{1,0:T(4,128)} %param.42) | copy-start | bytes 9220
  315.3 7.0 %collective-permute-start.7 = (f32[7,256]{1,0:T(8,128)S(1)}, f32[7,256]{1,0:T(8,128)S(1)}, u32[]{:S(2)}, u32[]{:S(2)}) collective-permute-start(f32[7,256]{1,0:T(8,128)S(1)} %pad_maximum_fusion), channel_id=1, source_target_pairs={{0,64},{64,128},{128,192},{192,256},{256,320},{320,384},{384,448},... | collective-permute-start | bytes 21512 | tf_op jit(solution)/shard_map/ppermute | solution.py:20
  322.3 7.0 %collective-permute-start.8 = (f32[7,256]{1,0:T(8,128)S(1)}, f32[7,256]{1,0:T(8,128)S(1)}, u32[]{:S(2)}, u32[]{:S(2)}) collective-permute-start(f32[7,256]{1,0:T(8,128)S(1)} %collective-permute-done.7), channel_id=1, source_target_pairs={{0,64},{64,128},{128,192},{192,256},{256,320},{320,384},{384,448},... | collective-permute-start | bytes 21512 | tf_op jit(solution)/shard_map/ppermute | solution.py:20
  329.4 7.5 %collective-permute-start.9 = (f32[7,256]{1,0:T(8,128)S(1)}, f32[7,256]{1,0:T(8,128)S(1)}, u32[]{:S(2)}, u32[]{:S(2)}) collective-permute-start(f32[7,256]{1,0:T(8,128)S(1)} %collective-permute-done.8), channel_id=1, source_target_pairs={{0,64},{64,128},{128,192},{192,256},{256,320},{320,384},{384,448},... | collective-permute-start | bytes 21512 | tf_op jit(solution)/shard_map/ppermute | solution.py:20
  336.8 9.1 %collective-permute-start.10 = (f32[7,256]{1,0:T(8,128)S(1)}, f32[7,256]{1,0:T(8,128)S(1)}, u32[]{:S(2)}, u32[]{:S(2)}) collective-permute-start(f32[7,256]{1,0:T(8,128)S(1)} %collective-permute-done.9), channel_id=1, source_target_pairs={{0,64},{64,128},{128,192},{192,256},{256,320},{320,384},{384,448},... | collective-permute-start | bytes 21512 | tf_op jit(solution)/shard_map/ppermute | solution.py:20
  346.0 21.0 %collective-permute-start.11 = (f32[7,256]{1,0:T(8,128)S(1)}, f32[7,256]{1,0:T(8,128)S(1)}, u32[]{:S(2)}, u32[]{:S(2)}) collective-permute-start(f32[7,256]{1,0:T(8,128)S(1)} %collective-permute-done.10), channel_id=1, source_target_pairs={{0,64},{64,128},{128,192},{192,256},{256,320},{320,384},{384,448},... | collective-permute-start | bytes 21512 | tf_op jit(solution)/shard_map/ppermute | solution.py:20
  354.8 26.5 %all-to-all-start.1 = ((f32[64,1,144]{2,1,0:T(1,128)}), f32[64,1,144]{2,1,0:T(1,128)S(1)}, u32[]{:S(2)}, u32[]{:S(2)}) async-start(f32[64,1,144]{2,1,0:T(1,128)} %reshape.341), calls=%async_computation.1 | async-start | bytes 131072 | tf_op jit(solution)/shard_map/all_to_all | solution.py:13
  367.0 7.2 %collective-permute-start.12 = (f32[7,256]{1,0:T(8,128)S(1)}, f32[7,256]{1,0:T(8,128)}, u32[]{:S(2)}, u32[]{:S(2)}) collective-permute-start(f32[7,256]{1,0:T(8,128)S(1)} %collective-permute-done.11), channel_id=1, source_target_pairs={{0,64},{64,128},{128,192},{192,256},{256,320},{320,384},{384,448},... | collective-permute-start | bytes 21512 | tf_op jit(solution)/shard_map/ppermute | solution.py:20
  374.2 39.1 %collective-permute-start.13 = (f32[7,256]{1,0:T(8,128)}, f32[7,256]{1,0:T(8,128)S(1)}, u32[]{:S(2)}, u32[]{:S(2)}) collective-permute-start(f32[7,256]{1,0:T(8,128)} %collective-permute-done.12), channel_id=1, source_target_pairs={{0,64},{64,128},{128,192},{192,256},{256,320},{320,384},{384,448},... | collective-permute-start | bytes 21512 | tf_op jit(solution)/shard_map/ppermute | solution.py:20
